TPU v7x, 256 devices: a whole 4x4x8 slice. The times are simulated.
256 devices in a mesh: acq: 16 (over z, core), tile: 16 (over y, x).
Axes of the slice: x: 4, y: 4, z: 8, core: 2. Of those that a mesh axis runs over, the one named last changes fastest.
Arguments:
- slc_tiles: bfloat16 [48, 2, 512, 2048], P('acq', None, 'tile'), may hold values from -64 to 64
- pair_first: int32 [768], P('acq'), may hold values from 0 to 47, as said below
- pair_second: int32 [768], P('acq'), may hold values from 0 to 47, as said below
- pair_signs: int32 [768, 2], P('acq'), may hold values from -1 to 1, as said below
- pair_counts: int32 [16], P('acq'), may hold values from 16 to 48, as said below
Outputs:
- right_side: float32 [48, 2, 512, 128], P('acq', None, 'tile')
Inputs may be any that keep to these rules, and one draw needn't show every extreme that they name: `pair_first`: the slots of index d of acq name as first acquisition only acquisitions 3 * d to 3 * d + 2. `pair_second`: A slot's second acquisition differs from its first. For every index d of acq and every other index s, all slots of d (live or not) whose second acquisition is owned by s name the same acquisition, and for every s other than d some live slot of d names one owned by s. `pair_signs`: each entry is -1 or 1. `pair_counts`: slots at positions from the count on are ignored. Every count is at least 16, and some index of acq has 48 in every draw.
All inputs are finite; a program needn't handle non-finite values.
Results may differ from a plain program's by a relative error of at most 0.0003.
Values may be sent and summed in bfloat16 or wider, within the bound.
A program may use at most 64 MiB of HBM per device.

v0:
```python
import jax
import jax.numpy as jnp
from jax import lax
from jax.sharding import PartitionSpec as P

LOOK_COLS = 16
LOOK_ROWS = 4


EPS = 1e-06


def with_halo(value, sides, width):
    for axis, dim in sides:
        count, length = (lax.axis_size(axis), value.shape[dim])
        up = [(i, (i + 1) % count) for i in range(count - 1)]
        down = [(j, i) for i, j in up]
        last = lax.slice_in_dim(value, length - width, length, axis=dim)
        initial = lax.slice_in_dim(value, 0, width, axis=dim)
        before = lax.ppermute(last, axis, up)
        after = lax.ppermute(initial, axis, down)
        value = jnp.concatenate([before, value, after], axis=dim)
    return value


def column_sums(candidates, first_rows, second_rows):
    col_count = candidates.shape[3]
    look_count = col_count // LOOK_COLS
    pooling = (
        (jnp.arange(col_count, dtype=jnp.int32) // LOOK_COLS)[:, None]
        == jnp.arange(look_count, dtype=jnp.int32)[None, :]
    ).astype(jnp.float32)

    def pooled(values):
        return jnp.einsum(
            "src,cl->srl",
            values,
            pooling,
            precision=lax.Precision.HIGHEST,
            preferred_element_type=jnp.float32,
        )

    def one_block(index_pair):
        left = jnp.take(candidates, index_pair[0], axis=0).astype(jnp.float32)
        right = jnp.take(candidates, index_pair[1], axis=0).astype(jnp.float32)
        left_real, left_imag = (left[:, 0], left[:, 1])
        right_real, right_imag = (right[:, 0], right[:, 1])
        return jnp.stack(
            [
                pooled(left_real * right_real + left_imag * right_imag),
                pooled(left_imag * right_real - left_real * right_imag),
                pooled(left_real * left_real + left_imag * left_imag),
                pooled(right_real * right_real + right_imag * right_imag),
            ],
            axis=1,
        )

    blocks = lax.map(one_block, (first_rows.reshape(-1, 8), second_rows.reshape(-1, 8)))
    return blocks.reshape((first_rows.shape[0],) + blocks.shape[2:])


def window_rows(padded, row_count):
    running = padded[:, :, 0:row_count]
    for offset in range(1, LOOK_ROWS):
        running = running + padded[:, :, offset : offset + row_count]
    return running


def body(slc_tiles, pair_first, pair_second, pair_signs, pair_counts):
    device_index = lax.axis_index("acq")
    acq_count = lax.axis_size("acq")
    owned_count = slc_tiles.shape[0]
    row_count = slc_tiles.shape[2]
    slot_count = pair_first.shape[0]
    half_window = LOOK_ROWS // 2
    first_owned = device_index * owned_count
    all_seconds = lax.all_gather(pair_second, "acq", axis=0, tiled=True).reshape(
        acq_count, slot_count
    )
    owned_mask = all_seconds // owned_count == device_index
    wanted = jnp.max(jnp.where(owned_mask, all_seconds - first_owned, 0), axis=1)
    local_stack = with_halo(slc_tiles, (("tile", 2),), half_window)
    outgoing = jnp.take(local_stack, wanted, axis=0)
    incoming = lax.all_to_all(outgoing, "acq", split_axis=0, concat_axis=0, tiled=True)
    candidates = jnp.concatenate([local_stack, incoming], axis=0)
    second_owner = pair_second // owned_count
    is_local = second_owner == device_index
    second_rows = jnp.where(is_local, pair_second - first_owned, owned_count + second_owner)
    first_rows = pair_first - first_owned
    sums = column_sums(candidates, first_rows, second_rows)
    boxed = window_rows(sums, row_count)
    scale_factor = lax.rsqrt(boxed[:, 2] * boxed[:, 3] + EPS)
    interferograms = jnp.stack([boxed[:, 0] * scale_factor, boxed[:, 1] * scale_factor], axis=1)
    item_shape = interferograms.shape[1:]
    flattened = interferograms.reshape(slot_count, -1)
    alive = (jnp.arange(slot_count) < pair_counts[0]).astype(jnp.float32)
    first_sign = pair_signs[:, 0].astype(jnp.float32) * alive
    second_sign = pair_signs[:, 1].astype(jnp.float32) * alive
    targets = jnp.arange(lax.axis_size("acq") * owned_count, dtype=jnp.int32)
    weights = first_sign[None, :] * (pair_first[None, :] == targets[:, None]).astype(jnp.float32)
    weights = weights + second_sign[None, :] * (pair_second[None, :] == targets[:, None]).astype(
        jnp.float32
    )
    summed = jnp.dot(
        weights, flattened, precision=lax.Precision.HIGHEST, preferred_element_type=jnp.float32
    )
    return lax.psum_scatter(
        summed.reshape((lax.axis_size("acq") * owned_count,) + item_shape),
        "acq",
        scatter_dimension=0,
        tiled=True,
    )


def solution(mesh):
    placed = (P("acq", None, "tile", None), P("acq"), P("acq"), P("acq", None), P("acq"))
    return jax.shard_map(
        body, mesh=mesh, in_specs=placed, out_specs=P("acq", None, "tile", None), check_vma=False
    )
```

profile of v0, /device:TPU:1, one launch (start us, length us, event | category | flops | bytes accessed | tf_op | source)
XLA Modules:
  0.0 406.2 jit_solution(2530121083609835278)
XLA Ops:
  7.7 3.9 collective-permute-start
  15.8 14.2 %all-reduce = s32[768]{0:T(1024)S(1)} all-reduce(s32[768]{0:T(1024)S(1)} %dynamic-update-slice), channel_id=1, replica_groups=mesh['acq'=16,'tile'=16] {'acq'}, use_global_device_ids=true, to_apply=%add | all-reduce | flops 768 | bytes 6144
  32.5 11.0 %gather_fusion.2 = bf16[16,2,36,2048]{3,1,2,0:T(2,128)(2,1)} fusion(bf16[3,2,36,2048]{3,1,2,0:T(2,128)(2,1)S(1)} %constant_dynamic-update-slice_fusion, s32[1024]{0:T(1024)S(1)} %pad_clamp_fusion.2), kind=kCustom, calls=%fused_computation.2 | custom fusion | bytes 9437248 | tf_op jit(solution)/shard_map/jit(_take)/gather | solution.py:83
  43.5 8.6 %broadcast_select_fusion = bf16[16,2,36,2048]{3,1,2,0:T(2,128)(2,1)} fusion(bf16[16,2,36,2048]{3,1,2,0:T(2,128)(2,1)} %gather_fusion.2, pred[16]{0:T(512)(128)(4,1)S(1)} %compare_and_fusion.2), kind=kLoop, calls=%fused_computation.67 | loop fusion | flops 2359296 | bytes 9437200 | tf_op jit(solution)/shard_map/jit(_take)/select_n | solution.py:83
  52.2 7.5 %all-to-all-start = ((bf16[16,2,36,2048]{3,1,2,0:T(2,128)(2,1)}), bf16[16,2,36,2048]{3,1,2,0:T(2,128)(2,1)}, u32[]{:S(2)}, u32[]{:S(2)}) async-start(bf16[16,2,36,2048]{3,1,2,0:T(2,128)(2,1)} %broadcast_select_fusion), calls=%async_computation | async-start | bytes 9437184 | tf_op jit(solution)/shard_map/all_to_all | solution.py:84
  60.8 103.8 %all-to-all-done = bf16[16,2,36,2048]{3,1,2,0:T(2,128)(2,1)} async-done(((bf16[16,2,36,2048]{3,1,2,0:T(2,128)(2,1)}), bf16[16,2,36,2048]{3,1,2,0:T(2,128)(2,1)}, u32[]{:S(2)}, u32[]{:S(2)}) %all-to-all-start) | async-done | bytes 4718624 | tf_op jit(solution)/shard_map/all_to_all | solution.py:84
  164.5 8.6 %pad_maximum_fusion = bf16[19,2,36,2048]{3,1,2,0:T(2,128)(2,1)S(1)} fusion(bf16[16,2,36,2048]{3,1,2,0:T(2,128)(2,1)} %all-to-all-done, bf16[3,2,36,2048]{3,1,2,0:T(2,128)(2,1)S(1)} %constant_dynamic-update-slice_fusion), kind=kLoop, calls=%fused_computation.68 | loop fusion | flops 2801664 | bytes 11206656 | tf_op jit(solution)/shard_map/concatenate | solution.py:85
  173.1 5.4 %copy.25 = bf16[19,2,36,2048]{3,2,1,0:T(8,128)(2,1)} copy(bf16[19,2,36,2048]{3,1,2,0:T(2,128)(2,1)S(1)} %pad_maximum_fusion) | data formatting | bytes 11206656
  178.5 152.7 %while.12 = (s32[]{:T(128)}, f32[6,8,4,36,128]{4,1,0,3,2:T(8,128)}, s32[6,8]{1,0:T(8,128)S(1)}, bf16[19,2,36,2048]{3,2,1,0:T(8,128)(2,1)}, s32[6,8]{1,0:T(8,128)S(1)}, /*index=5*/s32[2048]{0:T(1024)S(1)}, s32[]{:T(128)}) while((s32[]{:T(128)}, f32[6,8,4,36,128]{4,1,0,3,2:T(8,128)}, s32[6,8]{1,0:T(8,128)S(1)}, ...), condition=%wide.region_2.4_spmd.clone.clone, body=%wide.region_1.3_spmd.clone.clone.sunk | while | flops 3638216704 | bytes 70624160 | solution.py:58
  178.5 3.5 gather_fusion.1
  182.0 2.8 select_convert_fusion.5
  184.8 5.0 %gather_fusion = bf16[8,2,36,2048]{3,2,1,0:T(8,128)(2,1)} fusion(bf16[19,2,36,2048]{3,2,1,0:T(8,128)(2,1)} %get-tuple-element.181, s32[1024]{0:T(1024)S(1)} %pad_clamp_fusion.5), kind=kCustom, calls=%fused_computation.1.clone.clone.1 | custom fusion | bytes 4718624 | tf_op jit(solution)/shard_map/while/body/eval_jaxpr/jit(_take)/gather | solution.py:45
  195.4 2.6 fusion.104
  204.0 3.5 gather_fusion.1
  207.5 2.8 select_convert_fusion.5
  210.3 5.0 %gather_fusion = bf16[8,2,36,2048]{3,2,1,0:T(8,128)(2,1)} fusion(bf16[19,2,36,2048]{3,2,1,0:T(8,128)(2,1)} %get-tuple-element.181, s32[1024]{0:T(1024)S(1)} %pad_clamp_fusion.5), kind=kCustom, calls=%fused_computation.1.clone.clone.1 | custom fusion | bytes 4718624 | tf_op jit(solution)/shard_map/while/body/eval_jaxpr/jit(_take)/gather | solution.py:45
  229.5 3.5 gather_fusion.1
  232.9 2.8 select_convert_fusion.5
  235.8 5.0 %gather_fusion = bf16[8,2,36,2048]{3,2,1,0:T(8,128)(2,1)} fusion(bf16[19,2,36,2048]{3,2,1,0:T(8,128)(2,1)} %get-tuple-element.181, s32[1024]{0:T(1024)S(1)} %pad_clamp_fusion.5), kind=kCustom, calls=%fused_computation.1.clone.clone.1 | custom fusion | bytes 4718624 | tf_op jit(solution)/shard_map/while/body/eval_jaxpr/jit(_take)/gather | solution.py:45
  246.3 2.6 fusion.104
  254.9 3.5 gather_fusion.1
  258.4 2.8 select_convert_fusion.5
  261.2 5.0 %gather_fusion = bf16[8,2,36,2048]{3,2,1,0:T(8,128)(2,1)} fusion(bf16[19,2,36,2048]{3,2,1,0:T(8,128)(2,1)} %get-tuple-element.181, s32[1024]{0:T(1024)S(1)} %pad_clamp_fusion.5), kind=kCustom, calls=%fused_computation.1.clone.clone.1 | custom fusion | bytes 4718624 | tf_op jit(solution)/shard_map/while/body/eval_jaxpr/jit(_take)/gather | solution.py:45
  271.8 2.6 fusion.104
  280.4 3.5 gather_fusion.1
  283.9 2.8 select_convert_fusion.5
  286.7 5.0 %gather_fusion = bf16[8,2,36,2048]{3,2,1,0:T(8,128)(2,1)} fusion(bf16[19,2,36,2048]{3,2,1,0:T(8,128)(2,1)} %get-tuple-element.181, s32[1024]{0:T(1024)S(1)} %pad_clamp_fusion.5), kind=kCustom, calls=%fused_computation.1.clone.clone.1 | custom fusion | bytes 4718624 | tf_op jit(solution)/shard_map/while/body/eval_jaxpr/jit(_take)/gather | solution.py:45
  305.8 3.5 gather_fusion.1
  309.3 2.8 select_convert_fusion.5
  312.1 5.0 %gather_fusion = bf16[8,2,36,2048]{3,2,1,0:T(8,128)(2,1)} fusion(bf16[19,2,36,2048]{3,2,1,0:T(8,128)(2,1)} %get-tuple-element.181, s32[1024]{0:T(1024)S(1)} %pad_clamp_fusion.5), kind=kCustom, calls=%fused_computation.1.clone.clone.1 | custom fusion | bytes 4718624 | tf_op jit(solution)/shard_map/while/body/eval_jaxpr/jit(_take)/gather | solution.py:45
  331.2 6.1 %slice_add_fusion = f32[48,4,32,128]{3,0,2,1:T(8,128)S(1)} fusion(f32[48,4,36,128]{3,0,2,1:T(8,128)} %bitcast.107), kind=kLoop, calls=%fused_computation.69 | loop fusion | flops 2359296 | bytes 15728640 | tf_op jit(solution)/shard_map/add | solution.py:65
  343.3 56.1 %reduce-scatter.2.cloned.1.call-done = f32[3,2,32,128]{3,2,1,0:T(8,128)} async-done(((f32[48,2,32,128]{3,2,1,0:T(8,128)}), f32[3,2,32,128]{3,2,1,0:T(8,128)}) %reduce-scatter.2.cloned.1.call-update) | async-done | bytes 98320 | tf_op jit(solution)/shard_map/reduce_scatter | solution.py:107
  (130 shorter events, 90.2 us)
Async XLA Ops:
  7.7 22.7 %collective-permute-start = (bf16[3,2,2,2048]{3,1,2,0:T(2,128)(2,1)S(1)}, bf16[3,2,2,2048]{3,1,2,0:T(2,128)(2,1)S(1)}, u32[]{:S(2)}, u32[]{:S(2)}) collective-permute-start(bf16[3,2,2,2048]{3,1,2,0:T(2,128)(2,1)S(1)} %copy.40), channel_id=1, source_target_pairs={{0,1},{1,2},{2,3},{3,4},{4,5},{5,6},{6,7},{7,8},{8,9},{9,10},{10,1... | collective-permute-start | bytes 147464 | tf_op jit(solution)/shard_map/ppermute | solution.py:20
  11.7 20.8 %collective-permute-start.1 = (bf16[3,2,2,2048]{3,1,2,0:T(2,128)(2,1)S(1)}, bf16[3,2,2,2048]{3,1,2,0:T(2,128)(2,1)S(1)}, u32[]{:S(2)}, u32[]{:S(2)}) collective-permute-start(bf16[3,2,2,2048]{3,1,2,0:T(2,128)(2,1)S(1)} %copy.41), channel_id=1, source_target_pairs={{1,0},{2,1},{3,2},{4,3},{5,4},{6,5},{7,6},{8,7},{9,8},{10,9},{11,1... | collective-permute-start | bytes 147464 | tf_op jit(solution)/shard_map/ppermute | solution.py:21
  52.2 7.7 %copy-start = (s32[48]{0:T(128)S(1)}, s32[48]{0:T(128)}, u32[]{:S(2)}) copy-start(s32[48]{0:T(128)} %param.11) | copy-start | bytes 580
  52.2 7.8 %copy-start.2 = (s32[48]{0:T(128)S(1)}, s32[48]{0:T(128)}, u32[]{:S(2)}) copy-start(s32[48]{0:T(128)} %param.10) | copy-start | bytes 580
  52.2 8.6 %copy-start.1 = (s32[48,2]{0,1:T(2,128)S(1)}, s32[48,2]{0,1:T(2,128)}, u32[]{:S(2)}) copy-start(s32[48,2]{0,1:T(2,128)} %param.12) | copy-start | bytes 1156
  52.2 112.4 %all-to-all-start = ((bf16[16,2,36,2048]{3,1,2,0:T(2,128)(2,1)}), bf16[16,2,36,2048]{3,1,2,0:T(2,128)(2,1)}, u32[]{:S(2)}, u32[]{:S(2)}) async-start(bf16[16,2,36,2048]{3,1,2,0:T(2,128)(2,1)} %broadcast_select_fusion), calls=%async_computation | async-start | bytes 9437184 | tf_op jit(solution)/shard_map/all_to_all | solution.py:84
  59.7 339.7 %reduce-scatter.2.cloned.1.call-start = ((), (), s32[]{:S(2)}) async-start(), calls=%async_computation.2 | async-start | bytes 1671168 | tf_op jit(solution)/shard_map/reduce_scatter | solution.py:107
  184.8 7.3 %slice-start = ((s8[5242880]{0:T(1024)(128)(4,1)}), s8[1048576]{0:T(1024)(128)(4,1)S(1)}, s32[]{:S(2)}) async-start(s8[5242880]{0:T(1024)(128)(4,1)} %bitcast.105), calls=%async_computation.3 | async-start | bytes 2097152 | tf_op jit(solution)/shard_map/while
  189.9 3.0 slice-start.1
  210.3 7.3 %slice-start = ((s8[5242880]{0:T(1024)(128)(4,1)}), s8[1048576]{0:T(1024)(128)(4,1)S(1)}, s32[]{:S(2)}) async-start(s8[5242880]{0:T(1024)(128)(4,1)} %bitcast.105), calls=%async_computation.3 | async-start | bytes 2097152 | tf_op jit(solution)/shard_map/while
  215.3 3.0 slice-start.1
  235.8 7.3 %slice-start = ((s8[5242880]{0:T(1024)(128)(4,1)}), s8[1048576]{0:T(1024)(128)(4,1)S(1)}, s32[]{:S(2)}) async-start(s8[5242880]{0:T(1024)(128)(4,1)} %bitcast.105), calls=%async_computation.3 | async-start | bytes 2097152 | tf_op jit(solution)/shard_map/while
  240.8 3.0 slice-start.1
  261.2 7.3 %slice-start = ((s8[5242880]{0:T(1024)(128)(4,1)}), s8[1048576]{0:T(1024)(128)(4,1)S(1)}, s32[]{:S(2)}) async-start(s8[5242880]{0:T(1024)(128)(4,1)} %bitcast.105), calls=%async_computation.3 | async-start | bytes 2097152 | tf_op jit(solution)/shard_map/while
  266.2 3.0 slice-start.1
  286.7 7.3 %slice-start = ((s8[5242880]{0:T(1024)(128)(4,1)}), s8[1048576]{0:T(1024)(128)(4,1)S(1)}, s32[]{:S(2)}) async-start(s8[5242880]{0:T(1024)(128)(4,1)} %bitcast.105), calls=%async_computation.3 | async-start | bytes 2097152 | tf_op jit(solution)/shard_map/while
  291.7 3.0 slice-start.1
  312.1 7.3 %slice-start = ((s8[5242880]{0:T(1024)(128)(4,1)}), s8[1048576]{0:T(1024)(128)(4,1)S(1)}, s32[]{:S(2)}) async-start(s8[5242880]{0:T(1024)(128)(4,1)} %bitcast.105), calls=%async_computation.3 | async-start | bytes 2097152 | tf_op jit(solution)/shard_map/while
  317.1 3.0 slice-start.1
Sparse Core Ops, SparseCore 0:
  343.5 55.8 reduce-scatter.1
where the time goes:
time: 409 us; the launch traced here: 406 us
  waiting for transfers between devices  160 us (39%)
  local copies, waits for them, and re-layouts  86.8 us (21%)
  matrix products  62.4 us (15%)
  other arithmetic  54.8 us (13%)
  between operations  14.9 us (4%)
  blocking collectives  14.2 us (3%)
  starting transfers between devices  12.9 us (3%)
    all_to_all x1, waiting for transfers between devices, body(): lax.all_to_all(outgoing, 'acq', split_axis=0, concat_axis=0, tiled=True)  104 us
    dot_general x24, matrix products, pooled(): jnp.einsum('src,cl->srl', values, pooling, precision=lax.Precision.HIGHES...  60.1 us
    reduce_scatter x1, waiting for transfers between devices, body(): lax.psum_scatter(summed.reshape((lax.axis_size('acq') * owned_count,) + i...  56.1 us
    gather x6, local copies, waits for them, and re-layouts, one_block(): right = jnp.take(candidates, index_pair[1], axis=0).astype(jnp.float32)  30.2 us
    gather x6, local copies, waits for them, and re-layouts, one_block(): left = jnp.take(candidates, index_pair[0], axis=0).astype(jnp.float32)  20.9 us
    convert_element_type x6, other arithmetic, one_block(): left = jnp.take(candidates, index_pair[0], axis=0).astype(jnp.float32)  16.8 us
    unnamed x1, blocking collectives  14.2 us
    convert_element_type x6, other arithmetic, one_block(): right = jnp.take(candidates, index_pair[1], axis=0).astype(jnp.float32)  13.8 us
  transfers between devices with their start and end apart: 4, of which 2 were waited for; matrix products, arithmetic and copies ran while one was open for 1% of the time, Pallas kernels for 0%

commit v1 on v0

v1 whole, which is shorter than its diff:
```python
import functools

import jax
import jax.numpy as jnp
from jax import lax
from jax.experimental import pallas as pl
from jax.experimental.pallas import tpu as pltpu
from jax.sharding import PartitionSpec as P

MESH = pl.DeviceIdType.MESH
F32 = jnp.float32
BF16 = jnp.bfloat16
EPS = 1e-06

N = 16
OWN = 3
IMGS = N * OWN
ROWS = 32
HALF = 16
COLS = 128
LOOKS = 8
CAP = 48
OFFSETS = (8, 9, 7, 6, 10, 11, 5, 4, 12, 13, 3, 2, 14, 15, 1)


def iota(shape, dim):
    return lax.broadcasted_iota(jnp.int32, shape, dim)


def nt_dot(a, b):
    return lax.dot_general(a, b, (((1,), (1,)), ((), ())), preferred_element_type=F32)


def kernel(
    slc, first, second, signs, counts, out,
    land, slots, perm, images, grams, weights, sums, back, landed,
    own_sem, slot_send, slot_recv, send_sem, recv_sem, halo_send, halo_recv, back_send, back_recv,
):
    me = lax.axis_index("acq")
    tile = lax.axis_index("tile")
    up = lax.rem(tile + (N - 1), N)
    down = lax.rem(tile + 1, N)
    peers = [lax.rem(me + k, N) for k in OFFSETS]

    barrier = pltpu.get_barrier_semaphore()
    for p in peers:
        pl.semaphore_signal(barrier, inc=1, device_id={"acq": p}, device_id_type=MESH)
    for t in (up, down):
        pl.semaphore_signal(barrier, inc=1, device_id={"tile": t}, device_id_type=MESH)

    def block(chunk, p):
        return slc.at[:, :, pl.ds((1 - chunk) * HALF, HALF), pl.ds(pl.multiple_of(p * COLS, COLS), COLS)]

    own = [
        pltpu.make_async_copy(block(c, me), land.at[c, pl.ds(me * OWN, OWN)], own_sem.at[c])
        for c in range(2)
    ]
    for c in own:
        c.start()

    live = (iota((1, CAP), 1) < counts[0]).astype(F32)
    diagonal = iota((CAP, CAP), 0) == iota((CAP, CAP), 1)
    sign = signs[...].astype(F32)
    slots[me] = jnp.zeros((4, 128), F32)
    slots[me, 0:1, 0:CAP] = first[...].astype(F32)
    slots[me, 1:2, 0:CAP] = second[...].astype(F32)
    for k in range(2):
        row = jnp.sum(jnp.where(diagonal, sign[:, k : k + 1], 0.0), axis=0, keepdims=True)
        slots[me, 2 + k : 3 + k, 0:CAP] = row * live

    major, minor = iota((256, 256), 0), iota((256, 256), 1)
    swap = ((major >> 4) == (minor & 15)) & ((major & 15) == (minor >> 4))
    perm[...] = swap.astype(F32).astype(BF16)

    pl.semaphore_wait(barrier, len(OFFSETS) + 2)

    sends = []
    for chunk in range(2):
        for p in peers:
            sends.append(
                pltpu.make_async_remote_copy(
                    src_ref=block(chunk, p),
                    dst_ref=land.at[chunk, pl.ds(me * OWN, OWN)],
                    send_sem=send_sem.at[chunk, p],
                    recv_sem=recv_sem.at[chunk, me],
                    device_id={"acq": p},
                    device_id_type=MESH,
                )
            )
            sends[-1].start()
        if chunk == 0:
            for p in peers:
                sends.append(
                    pltpu.make_async_remote_copy(
                        src_ref=slots.at[me],
                        dst_ref=slots.at[me],
                        send_sem=slot_send.at[p],
                        recv_sem=slot_recv.at[me],
                        device_id={"acq": p},
                        device_id_type=MESH,
                    )
                )
                sends[-1].start()

    for p in peers:
        pltpu.make_async_copy(slots.at[p], slots.at[p], slot_recv.at[p]).wait()
    column = iota((128, 128), 0)
    second_half = column >= IMGS
    wanted = jnp.where(second_half, column - IMGS, column)
    wanted = jnp.where(column >= 2 * IMGS, -1, wanted).astype(F32)
    flip = jnp.where(second_half, -1.0, 1.0)
    image = iota((IMGS, 128), 0).astype(F32)
    weights[...] = jnp.zeros_like(weights)

    @pl.loop(0, N)
    def _(d):
        row = slots[d]
        a, b = row[0:1], row[1:2]
        left = jnp.concatenate([(image == b).astype(F32), (image == a).astype(F32)], axis=1)
        right = jnp.concatenate(
            [jnp.where(wanted == a, row[2:3], 0.0), jnp.where(wanted == b, row[3:4] * flip, 0.0)], axis=1
        )
        weights[...] += nt_dot(left.astype(BF16), right.astype(BF16))

    def regroup(chunk):
        for g in range(IMGS // 16):
            both = [
                land[chunk, 16 * g : 16 * g + 16, part].reshape(16 * HALF, COLS) for part in range(2)
            ]
            turned = jnp.dot(perm[...], jnp.concatenate(both, axis=1), preferred_element_type=F32)
            base = 2 + (1 - chunk) * HALF
            images[base : base + HALF, 16 * g : 16 * g + 16, :] = turned.astype(BF16).reshape(
                HALF, 16, 2 * COLS
            )

    look = (iota((IMGS, 2 * COLS), 1) & (COLS - 1)) >> 4

    def gram(row):
        x = images[row]
        other = jnp.concatenate([x[:, COLS:], -x[:, :COLS]], axis=1)
        right = jnp.concatenate([x, other, jnp.zeros((32, 2 * COLS), BF16)], axis=0)
        left = jnp.concatenate(
            [jnp.where(look == l, x, jnp.zeros_like(x)) for l in range(LOOKS)], axis=0
        )
        grams[row] = nt_dot(left, right)

    eye = iota((IMGS, 128), 0) == iota((IMGS, 128), 1)

    def windows(row):
        w = weights[...]
        for l in range(LOOKS):
            g = [grams[row + k, l * IMGS : (l + 1) * IMGS, :] for k in range(5)]
            middle = g[1] + g[2]
            for k, box in enumerate((g[0] + middle + g[3], middle + (g[3] + g[4]))):
                power = jnp.where(eye, box, 0.0)
                along = jnp.sum(power, axis=0, keepdims=True)
                along = along + pltpu.roll(along, IMGS, 1)
                across = jnp.sum(power, axis=1, keepdims=True)
                scaled = box * lax.rsqrt(along * across + EPS) * w
                sums[row + k, l : l + 1, :] = jnp.sum(scaled, axis=0, keepdims=True)

    def arrive(chunk):
        own[chunk].wait()
        for p in peers:
            here = land.at[chunk, pl.ds(p * OWN, OWN)]
            pltpu.make_async_copy(here, here, recv_sem.at[chunk, p]).wait()

    def halo(source, target, k, t):
        return pltpu.make_async_remote_copy(
            src_ref=images.at[source],
            dst_ref=images.at[target],
            send_sem=halo_send.at[k],
            recv_sem=halo_recv.at[k],
            device_id={"tile": t},
            device_id_type=MESH,
        )

    to_down = halo(pl.ds(ROWS, 2), pl.ds(0, 2), 0, down)
    to_up = halo(pl.ds(2, 1), pl.ds(ROWS + 2, 1), 1, up)

    arrive(0)
    regroup(0)
    to_down.start()

    @pl.loop(2 + HALF, 2 + ROWS)
    def _(row):
        gram(row)

    @pl.loop(9, 15)
    def _(pair):
        windows(2 * pair)

    arrive(1)
    regroup(1)
    to_up.start()
    to_down.wait_recv()
    above = images[0:2]
    images[0:2] = jnp.where(tile == 0, jnp.zeros_like(above), above)

    @pl.loop(0, 2 + HALF)
    def _(row):
        gram(row)

    @pl.loop(0, 9)
    def _(pair):
        windows(2 * pair)

    to_up.wait_recv()
    below = images[ROWS + 2]
    images[ROWS + 2] = jnp.where(tile == N - 1, jnp.zeros_like(below), below)
    gram(ROWS + 2)
    windows(ROWS - 2)

    goal, source = iota((128, 128), 0), iota((128, 128), 1)
    q = goal & 7
    part = (q >= OWN).astype(jnp.int32)
    chosen = part * IMGS + (goal >> 3) * OWN + (q - part * OWN)
    pick = ((chosen == source) & (q < 2 * OWN)).astype(F32).astype(BF16)
    for half in range(2):
        values = sums[half * HALF : (half + 1) * HALF].reshape(128, 128)
        total = jnp.zeros((128, 128), F32)
        for _ in range(3):
            piece = values.astype(BF16)
            values = values - piece.astype(F32)
            total = total + nt_dot(pick, piece)
        total = pltpu.roll(total, me * LOOKS, 1)
        back[:, :, half * 128 : (half + 1) * 128] = total.reshape(N, 8, 128)

    for p in peers:
        sends.append(
            pltpu.make_async_remote_copy(
                src_ref=back.at[p],
                dst_ref=landed.at[me],
                send_sem=back_send.at[p],
                recv_sem=back_recv.at[me],
                device_id={"acq": p},
                device_id_type=MESH,
            )
        )
        sends[-1].start()
    landed[me] = back[me]
    for p in peers:
        pltpu.make_async_copy(landed.at[p], landed.at[p], back_recv.at[p]).wait()

    group = iota((8, 128), 1) >> 3
    for half in range(2):
        pieces = [landed[j, :, half * 128 : (half + 1) * 128] for j in range(N)]
        for r8 in range(0, HALF, 8):
            rows = []
            for r in range(r8, r8 + 8):
                merged = pieces[0]
                for j in range(1, N):
                    merged = jnp.where(group == (j + r) % N, pieces[j], merged)
                rows.append(pltpu.roll(merged, (128 - LOOKS * r) % 128, 1) if r else merged)
            turned = jnp.swapaxes(jnp.stack(rows, axis=0), 0, 1)
            for q_index in range(2 * OWN):
                base = half * HALF + r8
                out[q_index % OWN, q_index // OWN, base : base + 8, :] = turned[q_index]

    for copy in sends:
        copy.wait_send()
    to_down.wait_send()
    to_up.wait_send()


def body(slc_tiles, pair_first, pair_second, pair_signs, pair_counts):
    vmem = pl.BlockSpec(memory_space=pltpu.VMEM)
    return pl.pallas_call(
        kernel,
        out_shape=jax.ShapeDtypeStruct((OWN, 2, ROWS, 128), F32),
        in_specs=[
            pl.BlockSpec(memory_space=pltpu.HBM),
            vmem,
            vmem,
            vmem,
            pl.BlockSpec(memory_space=pltpu.SMEM),
        ],
        out_specs=vmem,
        scratch_shapes=[
            pltpu.VMEM((2, IMGS, 2, HALF, COLS), BF16),
            pltpu.VMEM((N, 4, 128), F32),
            pltpu.VMEM((256, 256), BF16),
            pltpu.VMEM((ROWS + 3, IMGS, 2 * COLS), BF16),
            pltpu.VMEM((ROWS + 3, LOOKS * IMGS, 128), F32),
            pltpu.VMEM((IMGS, 128), F32),
            pltpu.VMEM((ROWS, LOOKS, 128), F32),
            pltpu.VMEM((N, 8, 256), F32),
            pltpu.VMEM((N, 8, 256), F32),
            pltpu.SemaphoreType.DMA((2,)),
            pltpu.SemaphoreType.DMA((N,)),
            pltpu.SemaphoreType.DMA((N,)),
            pltpu.SemaphoreType.DMA((2, N)),
            pltpu.SemaphoreType.DMA((2, N)),
            pltpu.SemaphoreType.DMA((2,)),
            pltpu.SemaphoreType.DMA((2,)),
            pltpu.SemaphoreType.DMA((N,)),
            pltpu.SemaphoreType.DMA((N,)),
        ],
        compiler_params=pltpu.CompilerParams(
            collective_id=0, has_side_effects=True, vmem_limit_bytes=40 * 1024 * 1024
        ),
    )(slc_tiles, pair_first.reshape(1, CAP), pair_second.reshape(1, CAP), pair_signs, pair_counts)


def solution(mesh):
    placed = (P("acq", None, "tile", None), P("acq"), P("acq"), P("acq", None), P("acq"))
    return jax.shard_map(
        body, mesh=mesh, in_specs=placed, out_specs=P("acq", None, "tile", None), check_vma=False
    )
```

time: 409 us -> 51.3 us (0.13)
  waiting for transfers between devices: 160 us -> 0 us
  local copies, waits for them, and re-layouts: 86.8 us -> 3.12 us
  matrix products: 62.4 us -> 0 us
  other arithmetic: 54.8 us -> 0 us
  Pallas kernels: 0 us -> 47.4 us
  between operations: 14.9 us -> 0.67 us
  blocking collectives: 14.2 us -> 0 us
  starting transfers between devices: 12.9 us -> 0 us
    all_to_all x1 -> x0, waiting for transfers between devices: 104 us -> none  [body(): lax.all_to_all(outgoing, 'acq', split_axis=0, concat_axis=0, tiled=True)]
    dot_general x25 -> x0, matrix products: 62.4 us -> none  [the longest x24 60.1 us: pooled(): jnp.einsum('src,cl->srl', values, pooling, precision=lax.Precision.HIGHES...]
    gather x13 -> x0, local copies, waits for them, and re-layouts: 62.1 us -> none  [the longest x6 30.2 us: one_block(): right = jnp.take(candidates, index_pair[1], axis=0).astype(jnp.float32)]
    reduce_scatter x1 -> x0, waiting for transfers between devices: 56.1 us -> none  [body(): lax.psum_scatter(summed.reshape((lax.axis_size('acq') * owned_count,) + i...]
    pallas_call x0 -> x1, Pallas kernels: none -> 47.4 us  [body(): pl.pallas_call(kernel, out_shape=jax.ShapeDtypeStruct((OWN, 2, ROWS, 128)...]
    convert_element_type x12 -> x0, other arithmetic: 30.6 us -> none  [the longest x6 16.8 us: one_block(): left = jnp.take(candidates, index_pair[0], axis=0).astype(jnp.float32)]
    unnamed x1 -> x0, blocking collectives: 14.2 us -> none
    select_n x4 -> x0, other arithmetic: 8.67 us -> none  [the longest x2 8.65 us: body(): outgoing = jnp.take(local_stack, wanted, axis=0)]
  transfers between devices with their start and end apart: 4 -> 0, of which waited for: 2 -> 0; matrix products, arithmetic and copies ran while one was open for 1% -> 0% of each run, Pallas kernels for 0% -> 0%
where the time goes in v1:
time: 51.3 us; the launch traced here: 51.2 us
  Pallas kernels  47.4 us (92%)
  local copies, waits for them, and re-layouts  3.12 us (6%)
  between operations  0.67 us (1%)
    pallas_call x1, Pallas kernels, body(): pl.pallas_call(kernel, out_shape=jax.ShapeDtypeStruct((OWN, 2, ROWS, 128)...  47.4 us
    unnamed x10, local copies, waits for them, and re-layouts  3.12 us

profile of v1, /device:TPU:1, one launch (start us, length us, event | category | flops | bytes accessed | tf_op | source)
XLA Modules:
  0.0 51.2 jit_solution(1677609006216346431)
XLA Ops:
  0.7 0.0 copy-start.3
  0.7 0.7 %copy-done.3 = s32[48,2]{0,1:T(2,128)S(1)} copy-done((s32[48,2]{0,1:T(2,128)S(1)}, s32[48,2]{0,1:T(2,128)}, u32[]{:S(2)}) %copy-start.3) | copy-done | bytes 408
  1.3 0.0 copy-start.1
  1.3 0.0 copy-start.2
  1.3 0.1 copy.6.signs
  1.4 0.6 %copy-done.1 = s32[48]{0:T(128)S(1)} copy-done((s32[48]{0:T(128)S(1)}, s32[48]{0:T(128)}, u32[]{:S(2)}) %copy-start.1) | copy-done | bytes 216
  2.0 0.0 copy-done.2
  2.0 0.0 copy-start
  2.0 1.1 %copy-done = bf16[3,2,32,2048]{3,2,1,0:T(8,128)(2,1)S(1)} copy-done((bf16[3,2,32,2048]{3,2,1,0:T(8,128)(2,1)S(1)}, bf16[3,2,32,2048]{3,2,1,0:T(8,128)(2,1)}, u32[]{:S(2)}) %copy-start) | copy-done | bytes 786456
  3.1 47.4 %shard_map.55 = f32[3,2,32,128]{3,2,1,0:T(8,128)S(1)} custom-call(bf16[3,2,32,2048]{3,2,1,0:T(8,128)(2,1)S(1)} %copy-done, s32[1,48]{1,0:T(1,128)S(1)} %bitcast.2, s32[1,48]{1,0:T(1,128)S(1)} %bitcast.3, s32[48,2]{1,0:T(8,128)S(1)} %copy.6.signs, s32[1]{0:T(128)S(6)} %copy.8.counts), custom_call_target="tpu_custom_call" | custom-call | tf_op jit(solution)/shard_map/pallas_call | solution.py:268
  50.6 0.6 %copy.9 = f32[3,2,32,128]{3,2,1,0:T(8,128)} copy(f32[3,2,32,128]{3,2,1,0:T(8,128)S(1)} %shard_map.55) | data formatting | bytes 196608
Async XLA Ops:
  0.7 0.7 %copy-start.3 = (s32[48,2]{0,1:T(2,128)S(1)}, s32[48,2]{0,1:T(2,128)}, u32[]{:S(2)}) copy-start(s32[48,2]{0,1:T(2,128)} %param.8) | copy-start | bytes 1156
  1.3 0.7 %copy-start.1 = (s32[48]{0:T(128)S(1)}, s32[48]{0:T(128)}, u32[]{:S(2)}) copy-start(s32[48]{0:T(128)} %param.6) | copy-start | bytes 580
  1.3 0.7 %copy-start.2 = (s32[48]{0:T(128)S(1)}, s32[48]{0:T(128)}, u32[]{:S(2)}) copy-start(s32[48]{0:T(128)} %param.7) | copy-start | bytes 580
  2.0 1.1 %copy-start = (bf16[3,2,32,2048]{3,2,1,0:T(8,128)(2,1)S(1)}, bf16[3,2,32,2048]{3,2,1,0:T(8,128)(2,1)}, u32[]{:S(2)}) copy-start(bf16[3,2,32,2048]{3,2,1,0:T(8,128)(2,1)} %slc.1) | copy-start | bytes 2359300

commit v2 on v1

v2 whole, which is shorter than its diff:
```python
import functools

import jax
import jax.numpy as jnp
from jax import lax
from jax.experimental import pallas as pl
from jax.experimental.pallas import tpu as pltpu
from jax.sharding import PartitionSpec as P

MESH = pl.DeviceIdType.MESH
F32 = jnp.float32
BF16 = jnp.bfloat16
EPS = 1e-06

N = 16
OWN = 3
IMGS = N * OWN
ROWS = 32
HALF = 16
BLOCK = 8
BLOCKS = ROWS // BLOCK
ORDER = (3, 0, 1, 2)
TILE_X = 4
FIRST = 10
COLS = 128
LOOKS = 8
CAP = 48
VMEM_LIMIT = 48 * 1024 * 1024
OFFSETS = (1, 15, 14, 2, 3, 13, 12, 4, 5, 11, 10, 6, 7, 9, 8)


def iota(shape, dim):
    return lax.broadcasted_iota(jnp.int32, shape, dim)


def nt_dot(a, b):
    return lax.dot_general(a, b, (((1,), (1,)), ((), ())), preferred_element_type=F32)


def kernel(
    slc, first, second, signs, counts, out,
    land, slots, perm, images, grams, cols, across, along, pool, spread_ones, weights, sums, back, landed,
    given, small_sem, own_sem, slot_send, slot_recv, send_sem, recv_sem, halo_send, halo_recv, ready,
    back_send, back_recv,
):
    me = lax.axis_index("acq")
    tile = lax.axis_index("tile")
    peers = [lax.rem(me + k, N) for k in OFFSETS]
    has_up, has_down = tile > 0, tile < N - 1
    opens, closes = lax.rem(tile, TILE_X) == 0, lax.rem(tile, TILE_X) == TILE_X - 1
    greeted_up, greeted_down = jnp.logical_not(opens), closes & has_down

    barrier = pltpu.get_barrier_semaphore()
    for p in peers:
        pl.semaphore_signal(barrier, inc=1, device_id={"acq": p}, device_id_type=MESH)

    @pl.when(jnp.logical_not(closes))
    def _():
        pl.semaphore_signal(barrier, inc=1, device_id={"tile": tile + 1}, device_id_type=MESH)

    @pl.when(opens & has_up)
    def _():
        pl.semaphore_signal(barrier, inc=1, device_id={"tile": tile - 1}, device_id_type=MESH)

    small = [
        pltpu.make_async_copy(first, given.at[0:1], small_sem.at[0]),
        pltpu.make_async_copy(second, given.at[1:2], small_sem.at[1]),
        pltpu.make_async_copy(signs, given.at[2:4], small_sem.at[2]),
    ]
    for c in small:
        c.start()

    def block(b, p):
        return slc.at[:, :, b, :, pl.ds(pl.multiple_of(p * COLS, COLS), COLS)]

    own = [
        pltpu.make_async_copy(block(b, me), land.at[b, pl.ds(me * OWN, OWN)], own_sem.at[b])
        for b in range(BLOCKS)
    ]
    for c in own:
        c.start()

    major, minor = iota((128, 128), 0), iota((128, 128), 1)
    swap = ((major >> 4) == (minor & 7)) & ((major & 15) == (minor >> 3))
    perm[...] = swap.astype(F32).astype(BF16)

    lane = iota((512, 128), 1)
    look_of = (iota((512, 128), 0) & (COLS - 1)) >> 4
    pool[...] = ((look_of == (lane & 7)) & (lane < 24)).astype(F32).astype(BF16)
    row = iota((128, LOOKS * 128), 0)
    spread_ones[...] = (((row & 7) == (iota((128, LOOKS * 128), 1) >> 7)) & (row < 24)).astype(F32).astype(BF16)

    for c in small:
        c.wait()
    numbers = given[...].astype(F32)
    live = (iota((4, CAP), 1) < counts[0]).astype(F32)
    numbers = jnp.where(iota((4, CAP), 0) >= 2, numbers * live, numbers)
    slots[me] = jnp.zeros((2, 128), F32)
    for k in range(2):
        for part in range(2):
            slots[me, k : k + 1, 64 * part : 64 * part + CAP] = numbers[2 * k + part : 2 * k + part + 1]

    greetings = greeted_up.astype(jnp.int32) + greeted_down.astype(jnp.int32)
    pl.semaphore_wait(barrier, len(OFFSETS) + greetings)

    @pl.when(greeted_up)
    def _():
        pl.semaphore_signal(ready.at[0], inc=1, device_id={"tile": tile - 1}, device_id_type=MESH)

    @pl.when(greeted_down)
    def _():
        pl.semaphore_signal(ready.at[1], inc=1, device_id={"tile": tile + 1}, device_id_type=MESH)

    sends = []

    def send(source, target, send_semaphore, recv_semaphore, p):
        copy = pltpu.make_async_remote_copy(
            src_ref=source,
            dst_ref=target,
            send_sem=send_semaphore,
            recv_sem=recv_semaphore,
            device_id={"acq": p},
            device_id_type=MESH,
        )
        copy.start()
        sends.append(copy)

    mine = pl.ds(me * OWN, OWN)
    for p in reversed(peers):
        send(slots.at[me], slots.at[me], slot_send.at[p], slot_recv.at[me], p)
    for b in ORDER:
        for p in peers:
            send(block(b, p), land.at[b, mine], send_sem.at[b, p], recv_sem.at[b, me], p)

    for p in peers:
        pltpu.make_async_copy(slots.at[p], slots.at[p], slot_recv.at[p]).wait()
    column = iota((128, 128), 0)
    second_half = column >= IMGS
    wanted = jnp.where(second_half, column - IMGS, column)
    wanted = jnp.where(column >= 2 * IMGS, -1, wanted).astype(F32)
    flip = jnp.where(second_half, -1.0, 1.0)
    image = iota((IMGS, 128), 0).astype(F32)
    weights[...] = jnp.zeros_like(weights)

    used = iota((1, 128), 1) < CAP

    @pl.loop(0, N // 4)
    def _(i):
        left, right = [], []
        for k in range(4):
            row = slots[4 * i + k]
            turned = pltpu.roll(row, 64, 1)
            a, b = row[0:1], turned[0:1]
            a_sign, b_sign = (jnp.where(used, v[1:2], 0.0) for v in (row, turned))
            left += [(image == b).astype(F32), (image == a).astype(F32)]
            right += [jnp.where(wanted == a, a_sign, 0.0), jnp.where(wanted == b, b_sign * flip, 0.0)]
        weights[...] += nt_dot(
            jnp.concatenate(left, axis=1).astype(BF16), jnp.concatenate(right, axis=1).astype(BF16)
        )

    def regroup(b):
        for g in range(IMGS // 16):
            both = [land[b, 16 * g : 16 * g + 16, part].reshape(16 * BLOCK, COLS) for part in range(2)]
            turned = jnp.dot(perm[...], jnp.concatenate(both, axis=1), preferred_element_type=F32)
            images[2 + BLOCK * b : 2 + BLOCK * (b + 1), 16 * g : 16 * g + 16, :] = turned.astype(
                BF16
            ).reshape(BLOCK, 16, 2 * COLS)

    look = (iota((IMGS, 2 * COLS), 1) & (COLS - 1)) >> 4

    def gram(row):
        x = images[row]
        other = jnp.concatenate([x[:, COLS:], -x[:, :COLS]], axis=1)
        right = jnp.concatenate([x, other, jnp.zeros((32, 2 * COLS), BF16)], axis=0)
        left = jnp.concatenate(
            [jnp.where(look == l, x, jnp.zeros_like(x)) for l in range(LOOKS)], axis=0
        )
        grams[row] = nt_dot(left, right)

    def power(row):
        x = images[row].astype(F32)
        square = x * x
        high = square.astype(BF16)
        low = (square - high.astype(F32)).astype(BF16)
        cols[row] = jnp.dot(jnp.concatenate([high, low], axis=1), pool[...], preferred_element_type=F32)

    copy_of = iota((IMGS, 128), 1) >> 3
    gather = iota((16, 128), 1)
    gather = (((gather & 7) == iota((16, 128), 0)) & (gather < 24)).astype(F32).astype(BF16)

    def spread(rows):
        split = []
        for row in rows:
            q = [cols[row + k] for k in range(4)]
            value = (q[0] + q[1]) + (q[2] + q[3])
            high = value.astype(BF16).astype(F32)
            value = value - high
            middle = value.astype(BF16).astype(F32)
            value = jnp.where(copy_of == 0, high, jnp.where(copy_of == 1, middle, value - middle))
            split.append(value.astype(BF16))
        wide = jnp.dot(jnp.concatenate(split, axis=0), spread_ones[...], preferred_element_type=F32)
        for k, row in enumerate(rows):
            across[row] = wide[k * IMGS : (k + 1) * IMGS]
            both = jnp.concatenate([split[k], split[k], jnp.zeros((32, 128), BF16)], axis=0)
            along[row] = nt_dot(gather, both)[0:LOOKS]

    def place(row):
        at = lax.rem(row + (ROWS - FIRST), ROWS)
        return (at & HALF) + ((at + me) & (HALF - 1))

    def windows(row):
        w = weights[...]
        for l in range(LOOKS):
            g = [grams[row + k, l * IMGS : (l + 1) * IMGS, :] for k in range(5)]
            middle = g[1] + g[2]
            for k, box in enumerate((g[0] + middle + g[3], middle + (g[3] + g[4]))):
                powers = along[row + k, l : l + 1] * across[row + k, :, l * 128 : (l + 1) * 128]
                scaled = box * lax.rsqrt(powers + EPS) * w
                sums[place(row + k), l : l + 1, :] = jnp.sum(scaled, axis=0, keepdims=True)

    def arrive(b):
        own[b].wait()
        for p in peers:
            here = land.at[b, pl.ds(p * OWN, OWN)]
            pltpu.make_async_copy(here, here, recv_sem.at[b, p]).wait()
        regroup(b)

    def rows_of(b):
        for k in range(BLOCK):
            gram(2 + BLOCK * b + k)
            power(2 + BLOCK * b + k)

    def pairs(start, count):
        @pl.loop(0, count)
        def _(i):
            windows(start + 2 * i)

    def halo(source, target, k, t):
        return pltpu.make_async_remote_copy(
            src_ref=images.at[source],
            dst_ref=images.at[target],
            send_sem=halo_send.at[k],
            recv_sem=halo_recv.at[k],
            device_id={"tile": t},
            device_id_type=MESH,
        )

    to_down = halo(pl.ds(ROWS, 2), pl.ds(0, 2), 0, tile + 1)
    to_up = halo(pl.ds(2, 1), pl.ds(ROWS + 2, 1), 1, tile - 1)

    arrive(3)

    @pl.when(jnp.logical_not(closes))
    def _():
        pl.semaphore_wait(ready.at[0], 1)

    @pl.when(has_down)
    def _():
        to_down.start()

    rows_of(3)
    spread([26, 27, 28, 29])
    pairs(26, 2)

    arrive(0)

    @pl.when(opens & has_up)
    def _():
        pl.semaphore_wait(ready.at[1], 1)

    @pl.when(has_up)
    def _():
        to_up.start()

    rows_of(0)
    spread([2, 3, 4, 5])
    pairs(2, 2)

    @pl.when(has_up)
    def _():
        to_down.wait_recv()

    @pl.when(tile == 0)
    def _():
        images[0:2] = jnp.zeros((2, IMGS, 2 * COLS), BF16)

    @pl.when(has_down)
    def _():
        to_up.wait_recv()

    @pl.when(tile == N - 1)
    def _():
        images[ROWS + 2] = jnp.zeros((IMGS, 2 * COLS), BF16)

    for row in (0, 1, ROWS + 2):
        gram(row)
        power(row)
    spread([0, 1, 30, 31])
    windows(0)
    windows(30)

    arrive(1)
    rows_of(1)
    spread([6, 7, 8, 9, 10, 11, 12, 13])
    pairs(6, 4)

    goal, source = iota((128, 384), 0), iota((128, 384), 1) & 127
    q = goal & 7
    part = (q >= OWN).astype(jnp.int32)
    chosen = part * IMGS + (goal >> 3) * OWN + (q - part * OWN)
    pick = ((chosen == source) & (q < 2 * OWN)).astype(F32).astype(BF16)

    def give(half):
        values = sums[half * HALF : (half + 1) * HALF].reshape(128, 128)
        pieces = []
        for _ in range(3):
            pieces.append(values.astype(BF16))
            values = values - pieces[-1].astype(F32)
        total = nt_dot(pick, jnp.concatenate(pieces, axis=1))
        back[half] = total.reshape(N, 8, 128)[:, : 2 * OWN]
        for p in reversed(peers):
            send(back.at[half, p], landed.at[half, me], back_send.at[half, p], back_recv.at[half, me], p)
        landed[half, me] = back[half, me]

    group = iota((2 * OWN, 128), 1) >> 3

    def take(half):
        for p in peers:
            here = landed.at[half, p]
            pltpu.make_async_copy(here, here, back_recv.at[half, p]).wait()
        pieces = [landed[half, j] for j in range(N)]
        for r8 in range(0, HALF, 8):
            rows = []
            for r in range(r8, r8 + 8):
                merged = pieces[0]
                for j in range(1, N):
                    merged = jnp.where(group == (j + r) % N, pieces[j], merged)
                rows.append(pltpu.roll(merged, (128 - LOOKS * r) % 128, 1) if r else merged)
            turned = jnp.swapaxes(jnp.stack(rows, axis=0), 0, 1)
            start = (FIRST + half * HALF + r8) % ROWS
            size = min(8, ROWS - start)
            for k in range(2 * OWN):
                out[k % OWN, k // OWN, start : start + size, :] = turned[k, :size]
                if size < 8:
                    out[k % OWN, k // OWN, 0 : 8 - size, :] = turned[k, size:]

    arrive(2)
    give(1)
    rows_of(2)
    spread([14, 15, 16, 17, 18, 19])
    spread([20, 21, 22, 23, 24, 25])
    pairs(14, 6)
    give(0)
    take(1)
    take(0)

    for copy in sends:
        copy.wait_send()

    @pl.when(has_down)
    def _():
        to_down.wait_send()

    @pl.when(has_up)
    def _():
        to_up.wait_send()


def body(slc_tiles, pair_first, pair_second, pair_signs, pair_counts):
    vmem = pl.BlockSpec(memory_space=pltpu.VMEM)
    return pl.pallas_call(
        kernel,
        out_shape=jax.ShapeDtypeStruct((OWN, 2, ROWS, 128), F32),
        in_specs=[pl.BlockSpec(memory_space=pltpu.HBM)] * 4 + [pl.BlockSpec(memory_space=pltpu.SMEM)],
        out_specs=vmem,
        scratch_shapes=[
            pltpu.VMEM((BLOCKS, IMGS, 2, BLOCK, COLS), BF16),
            pltpu.VMEM((N, 2, 128), F32),
            pltpu.VMEM((128, 128), BF16),
            pltpu.VMEM((ROWS + 3, IMGS, 2 * COLS), BF16),
            pltpu.VMEM((ROWS + 3, LOOKS * IMGS, 128), F32),
            pltpu.VMEM((ROWS + 3, IMGS, 128), F32),
            pltpu.VMEM((ROWS, IMGS, LOOKS * 128), F32),
            pltpu.VMEM((ROWS, LOOKS, 128), F32),
            pltpu.VMEM((512, 128), BF16),
            pltpu.VMEM((128, LOOKS * 128), BF16),
            pltpu.VMEM((IMGS, 128), F32),
            pltpu.VMEM((ROWS, LOOKS, 128), F32),
            pltpu.VMEM((2, N, 2 * OWN, 128), F32),
            pltpu.VMEM((2, N, 2 * OWN, 128), F32),
            pltpu.VMEM((4, CAP), jnp.int32),
            pltpu.SemaphoreType.DMA((3,)),
            pltpu.SemaphoreType.DMA((BLOCKS,)),
            pltpu.SemaphoreType.DMA((N,)),
            pltpu.SemaphoreType.DMA((N,)),
            pltpu.SemaphoreType.DMA((BLOCKS, N)),
            pltpu.SemaphoreType.DMA((BLOCKS, N)),
            pltpu.SemaphoreType.DMA((2,)),
            pltpu.SemaphoreType.DMA((2,)),
            pltpu.SemaphoreType.REGULAR((2,)),
            pltpu.SemaphoreType.DMA((2, N)),
            pltpu.SemaphoreType.DMA((2, N)),
        ],
        compiler_params=pltpu.CompilerParams(
            collective_id=0, has_side_effects=True, vmem_limit_bytes=VMEM_LIMIT
        ),
    )(
        *(
            pltpu.with_memory_space_constraint(v, pltpu.HBM)
            for v in (
                slc_tiles.reshape(OWN, 2, BLOCKS, BLOCK, N * COLS),
                pair_first.reshape(1, CAP),
                pair_second.reshape(1, CAP),
                pair_signs.T,
            )
        ),
        pair_counts,
    )


def solution(mesh):
    placed = (P("acq", None, "tile", None), P("acq"), P("acq"), P("acq", None), P("acq"))
    return jax.shard_map(
        body, mesh=mesh, in_specs=placed, out_specs=P("acq", None, "tile", None), check_vma=False
    )
```

time: 51.3 us -> 40 us (0.78)
  Pallas kernels: 47.4 us -> 38.6 us
  local copies, waits for them, and re-layouts: 3.12 us -> 0.64 us
    pallas_call x1, Pallas kernels: 47.4 us -> 38.6 us  [body(): pl.pallas_call(kernel, out_shape=jax.ShapeDtypeStruct((OWN, 2, ROWS, 128)...]
    unnamed x10 -> x1, local copies, waits for them, and re-layouts: 3.12 us -> 0.64 us
where the time goes in v2:
time: 40 us; the launch traced here: 39.9 us
  Pallas kernels  38.6 us (96%)
  between operations  0.66 us (2%)
  local copies, waits for them, and re-layouts  0.64 us (2%)
    pallas_call x1, Pallas kernels, body(): pl.pallas_call(kernel, out_shape=jax.ShapeDtypeStruct((OWN, 2, ROWS, 128)...  38.6 us

profile of v2, /device:TPU:1, one launch (start us, length us, event | category | flops | bytes accessed | tf_op | source)
XLA Modules:
  0.0 39.9 jit_solution(7033303770903030498)
XLA Ops:
  0.7 38.6 %shard_map.55 = f32[3,2,32,128]{3,2,1,0:T(8,128)S(1)} custom-call(bf16[3,2,4,8,2048]{4,3,2,1,0:T(8,128)(2,1)} %bitcast.4, s32[1,48]{1,0:T(1,128)} %bitcast.6, s32[1,48]{1,0:T(1,128)} %bitcast.7, s32[2,48]{1,0:T(2,128)} %bitcast.5, s32[1]{0:T(128)S(6)} %copy.7.counts), custom_call_target="tpu_custom_call" | custom-call | tf_op jit(solution)/shard_map/pallas_call | solution.py:371
  39.2 0.6 %copy.8 = f32[3,2,32,128]{3,2,1,0:T(8,128)} copy(f32[3,2,32,128]{3,2,1,0:T(8,128)S(1)} %shard_map.55) | data formatting | bytes 196608

commit v3 on v2

--- a/solution.py
+++ b/solution.py
@@ -80,26 +80,6 @@
     for c in own:
         c.start()
 
-    major, minor = iota((128, 128), 0), iota((128, 128), 1)
-    swap = ((major >> 4) == (minor & 7)) & ((major & 15) == (minor >> 3))
-    perm[...] = swap.astype(F32).astype(BF16)
-
-    lane = iota((512, 128), 1)
-    look_of = (iota((512, 128), 0) & (COLS - 1)) >> 4
-    pool[...] = ((look_of == (lane & 7)) & (lane < 24)).astype(F32).astype(BF16)
-    row = iota((128, LOOKS * 128), 0)
-    spread_ones[...] = (((row & 7) == (iota((128, LOOKS * 128), 1) >> 7)) & (row < 24)).astype(F32).astype(BF16)
-
-    for c in small:
-        c.wait()
-    numbers = given[...].astype(F32)
-    live = (iota((4, CAP), 1) < counts[0]).astype(F32)
-    numbers = jnp.where(iota((4, CAP), 0) >= 2, numbers * live, numbers)
-    slots[me] = jnp.zeros((2, 128), F32)
-    for k in range(2):
-        for part in range(2):
-            slots[me, k : k + 1, 64 * part : 64 * part + CAP] = numbers[2 * k + part : 2 * k + part + 1]
-
     greetings = greeted_up.astype(jnp.int32) + greeted_down.astype(jnp.int32)
     pl.semaphore_wait(barrier, len(OFFSETS) + greetings)
 
@@ -110,8 +90,6 @@
     @pl.when(greeted_down)
     def _():
         pl.semaphore_signal(ready.at[1], inc=1, device_id={"tile": tile + 1}, device_id_type=MESH)
-
-    sends = []
 
     def send(source, target, send_semaphore, recv_semaphore, p):
         copy = pltpu.make_async_remote_copy(
@@ -123,40 +101,41 @@
             device_id_type=MESH,
         )
         copy.start()
-        sends.append(copy)
+
+    def all_of(copies, semaphore):
+        pltpu.make_async_copy(copies, copies, semaphore).wait()
 
     mine = pl.ds(me * OWN, OWN)
+    def send_block(b):
+        for p in reversed(peers) if b == ORDER[-1] else peers:
+            send(block(b, p), land.at[b, mine], send_sem.at[b], recv_sem.at[b], p)
+
+    send_block(ORDER[0])
+
+    for c in small:
+        c.wait()
+    numbers = given[...].astype(F32)
+    live = (iota((4, CAP), 1) < counts[0]).astype(F32)
+    numbers = jnp.where(iota((4, CAP), 0) >= 2, numbers * live, numbers)
+    slots[me] = jnp.zeros((2, 128), F32)
+    for k in range(2):
+        for part in range(2):
+            slots[me, k : k + 1, 64 * part : 64 * part + CAP] = numbers[2 * k + part : 2 * k + part + 1]
+
     for p in reversed(peers):
-        send(slots.at[me], slots.at[me], slot_send.at[p], slot_recv.at[me], p)
-    for b in ORDER:
-        for p in peers:
-            send(block(b, p), land.at[b, mine], send_sem.at[b, p], recv_sem.at[b, me], p)
-
-    for p in peers:
-        pltpu.make_async_copy(slots.at[p], slots.at[p], slot_recv.at[p]).wait()
-    column = iota((128, 128), 0)
-    second_half = column >= IMGS
-    wanted = jnp.where(second_half, column - IMGS, column)
-    wanted = jnp.where(column >= 2 * IMGS, -1, wanted).astype(F32)
-    flip = jnp.where(second_half, -1.0, 1.0)
-    image = iota((IMGS, 128), 0).astype(F32)
-    weights[...] = jnp.zeros_like(weights)
-
-    used = iota((1, 128), 1) < CAP
-
-    @pl.loop(0, N // 4)
-    def _(i):
-        left, right = [], []
-        for k in range(4):
-            row = slots[4 * i + k]
-            turned = pltpu.roll(row, 64, 1)
-            a, b = row[0:1], turned[0:1]
-            a_sign, b_sign = (jnp.where(used, v[1:2], 0.0) for v in (row, turned))
-            left += [(image == b).astype(F32), (image == a).astype(F32)]
-            right += [jnp.where(wanted == a, a_sign, 0.0), jnp.where(wanted == b, b_sign * flip, 0.0)]
-        weights[...] += nt_dot(
-            jnp.concatenate(left, axis=1).astype(BF16), jnp.concatenate(right, axis=1).astype(BF16)
-        )
+        send(slots.at[me], slots.at[me], slot_send, slot_recv, p)
+    for b in ORDER[1:]:
+        send_block(b)
+
+    major, minor = iota((128, 128), 0), iota((128, 128), 1)
+    swap = ((major >> 4) == (minor & 7)) & ((major & 15) == (minor >> 3))
+    perm[...] = swap.astype(F32).astype(BF16)
+
+    lane = iota((512, 128), 1)
+    look_of = (iota((512, 128), 0) & (COLS - 1)) >> 4
+    pool[...] = ((look_of == (lane & 7)) & (lane < 24)).astype(F32).astype(BF16)
+    row = iota((128, LOOKS * 128), 0)
+    spread_ones[...] = (((row & 7) == (iota((128, LOOKS * 128), 1) >> 7)) & (row < 24)).astype(F32).astype(BF16)
 
     def regroup(b):
         for g in range(IMGS // 16):
@@ -220,9 +199,7 @@
 
     def arrive(b):
         own[b].wait()
-        for p in peers:
-            here = land.at[b, pl.ds(p * OWN, OWN)]
-            pltpu.make_async_copy(here, here, recv_sem.at[b, p]).wait()
+        all_of(land.at[b, pl.ds(0, (N - 1) * OWN)], recv_sem.at[b])
         regroup(b)
 
     def rows_of(b):
@@ -260,6 +237,33 @@
 
     rows_of(3)
     spread([26, 27, 28, 29])
+
+    others = pl.ds(0, N - 1)
+    all_of(slots.at[others], slot_recv)
+    column = iota((128, 128), 0)
+    second_half = column >= IMGS
+    wanted = jnp.where(second_half, column - IMGS, column)
+    wanted = jnp.where(column >= 2 * IMGS, -1, wanted).astype(F32)
+    flip = jnp.where(second_half, -1.0, 1.0)
+    image = iota((IMGS, 128), 0).astype(F32)
+    weights[...] = jnp.zeros_like(weights)
+
+    used = iota((1, 128), 1) < CAP
+
+    @pl.loop(0, N // 4)
+    def _(i):
+        left, right = [], []
+        for k in range(4):
+            row = slots[4 * i + k]
+            turned = pltpu.roll(row, 64, 1)
+            a, b = row[0:1], turned[0:1]
+            a_sign, b_sign = (jnp.where(used, v[1:2], 0.0) for v in (row, turned))
+            left += [(image == b).astype(F32), (image == a).astype(F32)]
+            right += [jnp.where(wanted == a, a_sign, 0.0), jnp.where(wanted == b, b_sign * flip, 0.0)]
+        weights[...] += nt_dot(
+            jnp.concatenate(left, axis=1).astype(BF16), jnp.concatenate(right, axis=1).astype(BF16)
+        )
+
     pairs(26, 2)
 
     arrive(0)
@@ -310,7 +314,7 @@
     chosen = part * IMGS + (goal >> 3) * OWN + (q - part * OWN)
     pick = ((chosen == source) & (q < 2 * OWN)).astype(F32).astype(BF16)
 
-    def give(half):
+    def turn(half):
         values = sums[half * HALF : (half + 1) * HALF].reshape(128, 128)
         pieces = []
         for _ in range(3):
@@ -318,16 +322,16 @@
             values = values - pieces[-1].astype(F32)
         total = nt_dot(pick, jnp.concatenate(pieces, axis=1))
         back[half] = total.reshape(N, 8, 128)[:, : 2 * OWN]
+
+    def give(half):
         for p in reversed(peers):
-            send(back.at[half, p], landed.at[half, me], back_send.at[half, p], back_recv.at[half, me], p)
+            send(back.at[half, p], landed.at[half, me], back_send.at[half], back_recv.at[half], p)
         landed[half, me] = back[half, me]
 
     group = iota((2 * OWN, 128), 1) >> 3
 
     def take(half):
-        for p in peers:
-            here = landed.at[half, p]
-            pltpu.make_async_copy(here, here, back_recv.at[half, p]).wait()
+        all_of(landed.at[half, others], back_recv.at[half])
         pieces = [landed[half, j] for j in range(N)]
         for r8 in range(0, HALF, 8):
             rows = []
@@ -344,18 +348,19 @@
                 if size < 8:
                     out[k % OWN, k // OWN, 0 : 8 - size, :] = turned[k, size:]
 
+    turn(1)
     arrive(2)
     give(1)
     rows_of(2)
     spread([14, 15, 16, 17, 18, 19])
     spread([20, 21, 22, 23, 24, 25])
     pairs(14, 6)
+    turn(0)
     give(0)
-    take(1)
-    take(0)
-
-    for copy in sends:
-        copy.wait_send()
+
+    all_of(slots.at[others], slot_send)
+    for b in ORDER:
+        all_of(land.at[b, pl.ds(0, (N - 1) * OWN)], send_sem.at[b])
 
     @pl.when(has_down)
     def _():
@@ -364,6 +369,10 @@
     @pl.when(has_up)
     def _():
         to_up.wait_send()
+
+    for half in (1, 0):
+        take(half)
+        all_of(back.at[half, others], back_send.at[half])
 
 
 def body(slc_tiles, pair_first, pair_second, pair_signs, pair_counts):
@@ -391,15 +400,15 @@
             pltpu.VMEM((4, CAP), jnp.int32),
             pltpu.SemaphoreType.DMA((3,)),
             pltpu.SemaphoreType.DMA((BLOCKS,)),
-            pltpu.SemaphoreType.DMA((N,)),
-            pltpu.SemaphoreType.DMA((N,)),
-            pltpu.SemaphoreType.DMA((BLOCKS, N)),
-            pltpu.SemaphoreType.DMA((BLOCKS, N)),
+            pltpu.SemaphoreType.DMA,
+            pltpu.SemaphoreType.DMA,
+            pltpu.SemaphoreType.DMA((BLOCKS,)),
+            pltpu.SemaphoreType.DMA((BLOCKS,)),
             pltpu.SemaphoreType.DMA((2,)),
             pltpu.SemaphoreType.DMA((2,)),
             pltpu.SemaphoreType.REGULAR((2,)),
-            pltpu.SemaphoreType.DMA((2, N)),
-            pltpu.SemaphoreType.DMA((2, N)),
+            pltpu.SemaphoreType.DMA((2,)),
+            pltpu.SemaphoreType.DMA((2,)),
         ],
         compiler_params=pltpu.CompilerParams(
             collective_id=0, has_side_effects=True, vmem_limit_bytes=VMEM_LIMIT

time: 40 us -> 37.5 us (0.938)
  Pallas kernels: 38.6 us -> 36.1 us
    pallas_call x1, Pallas kernels: 38.6 us -> 36.1 us  [body(): pl.pallas_call(kernel, out_shape=jax.ShapeDtypeStruct((OWN, 2, ROWS, 128)...]
where the time goes in v3:
time: 37.5 us; the launch traced here: 37.4 us
  Pallas kernels  36.1 us (96%)
  between operations  0.66 us (2%)
  local copies, waits for them, and re-layouts  0.64 us (2%)
    pallas_call x1, Pallas kernels, body(): pl.pallas_call(kernel, out_shape=jax.ShapeDtypeStruct((OWN, 2, ROWS, 128)...  36.1 us

profile of v3, /device:TPU:1, one launch (start us, length us, event | category | flops | bytes accessed | tf_op | source)
XLA Modules:
  0.0 37.4 jit_solution(13310274304923583196)
XLA Ops:
  0.7 36.1 %shard_map.55 = f32[3,2,32,128]{3,2,1,0:T(8,128)S(1)} custom-call(bf16[3,2,4,8,2048]{4,3,2,1,0:T(8,128)(2,1)} %bitcast.4, s32[1,48]{1,0:T(1,128)} %bitcast.6, s32[1,48]{1,0:T(1,128)} %bitcast.7, s32[2,48]{1,0:T(2,128)} %bitcast.5, s32[1]{0:T(128)S(6)} %copy.7.counts), custom_call_target="tpu_custom_call" | custom-call | tf_op jit(solution)/shard_map/pallas_call | solution.py:380
  36.7 0.6 %copy.8 = f32[3,2,32,128]{3,2,1,0:T(8,128)} copy(f32[3,2,32,128]{3,2,1,0:T(8,128)S(1)} %shard_map.55) | data formatting | bytes 196608

commit v4 on v3

--- a/solution.py
+++ b/solution.py
@@ -354,7 +354,8 @@
     rows_of(2)
     spread([14, 15, 16, 17, 18, 19])
     spread([20, 21, 22, 23, 24, 25])
-    pairs(14, 6)
+    for row in range(14, 26, 2):
+        windows(row)
     turn(0)
     give(0)
 

time: 37.5 us -> 36.9 us (0.984)
  Pallas kernels: 36.1 us -> 35.5 us
    pallas_call x1, Pallas kernels: 36.1 us -> 35.5 us  [body(): pl.pallas_call(kernel, out_shape=jax.ShapeDtypeStruct((OWN, 2, ROWS, 128)...]
where the time goes in v4:
time: 36.9 us
  Pallas kernels  35.5 us (96%)
  between operations  0.66 us (2%)
  local copies, waits for them, and re-layouts  0.64 us (2%)
    pallas_call x1, Pallas kernels, body(): pl.pallas_call(kernel, out_shape=jax.ShapeDtypeStruct((OWN, 2, ROWS, 128)...  35.5 us

profile of v4, /device:TPU:1, one launch (start us, length us, event | category | flops | bytes accessed | tf_op | source)
XLA Modules:
  0.0 36.9 jit_solution(10407114789906219603)
XLA Ops:
  0.7 35.5 %shard_map.55 = f32[3,2,32,128]{3,2,1,0:T(8,128)S(1)} custom-call(bf16[3,2,4,8,2048]{4,3,2,1,0:T(8,128)(2,1)} %bitcast.4, s32[1,48]{1,0:T(1,128)} %bitcast.6, s32[1,48]{1,0:T(1,128)} %bitcast.7, s32[2,48]{1,0:T(2,128)} %bitcast.5, s32[1]{0:T(128)S(6)} %copy.7.counts), custom_call_target="tpu_custom_call" | custom-call | tf_op jit(solution)/shard_map/pallas_call | solution.py:381
  36.2 0.6 %copy.8 = f32[3,2,32,128]{3,2,1,0:T(8,128)} copy(f32[3,2,32,128]{3,2,1,0:T(8,128)S(1)} %shard_map.55) | data formatting | bytes 196608

commit v5 on v4

--- a/solution.py
+++ b/solution.py
@@ -40,7 +40,7 @@
 def kernel(
     slc, first, second, signs, counts, out,
     land, slots, perm, images, grams, cols, across, along, pool, spread_ones, weights, sums, back, landed,
-    given, small_sem, own_sem, slot_send, slot_recv, send_sem, recv_sem, halo_send, halo_recv, ready,
+    stage, stage_sem, given, small_sem, own_sem, slot_send, slot_recv, send_sem, recv_sem, halo_send, halo_recv, ready,
     back_send, back_recv,
 ):
     me = lax.axis_index("acq")
@@ -70,16 +70,19 @@
     for c in small:
         c.start()
 
+    staged = [
+        pltpu.make_async_copy(slc.at[:, :, b], stage.at[:, :, b], stage_sem.at[b]) for b in range(BLOCKS)
+    ]
+    for b in ORDER:
+        staged[b].start()
+
     def block(b, p):
-        return slc.at[:, :, b, :, pl.ds(pl.multiple_of(p * COLS, COLS), COLS)]
+        return stage.at[:, :, b, :, pl.ds(pl.multiple_of(p * COLS, COLS), COLS)]
 
     own = [
         pltpu.make_async_copy(block(b, me), land.at[b, pl.ds(me * OWN, OWN)], own_sem.at[b])
         for b in range(BLOCKS)
     ]
-    for c in own:
-        c.start()
-
     greetings = greeted_up.astype(jnp.int32) + greeted_down.astype(jnp.int32)
     pl.semaphore_wait(barrier, len(OFFSETS) + greetings)
 
@@ -107,6 +110,8 @@
 
     mine = pl.ds(me * OWN, OWN)
     def send_block(b):
+        staged[b].wait()
+        own[b].start()
         for p in reversed(peers) if b == ORDER[-1] else peers:
             send(block(b, p), land.at[b, mine], send_sem.at[b], recv_sem.at[b], p)
 
@@ -398,6 +403,8 @@
             pltpu.VMEM((ROWS, LOOKS, 128), F32),
             pltpu.VMEM((2, N, 2 * OWN, 128), F32),
             pltpu.VMEM((2, N, 2 * OWN, 128), F32),
+            pltpu.VMEM((OWN, 2, BLOCKS, BLOCK, N * COLS), BF16),
+            pltpu.SemaphoreType.DMA((BLOCKS,)),
             pltpu.VMEM((4, CAP), jnp.int32),
             pltpu.SemaphoreType.DMA((3,)),
             pltpu.SemaphoreType.DMA((BLOCKS,)),

time: 36.9 us -> 36.8 us (level)
  no operation moved by 1% of the time
where the time goes in v5:
time: 36.8 us; the launch traced here: 36.7 us
  Pallas kernels  35.4 us (96%)
  between operations  0.66 us (2%)
  local copies, waits for them, and re-layouts  0.64 us (2%)
    pallas_call x1, Pallas kernels, body(): pl.pallas_call(kernel, out_shape=jax.ShapeDtypeStruct((OWN, 2, ROWS, 128)...  35.4 us

profile of v5, /device:TPU:1, one launch (start us, length us, event | category | flops | bytes accessed | tf_op | source)
XLA Modules:
  0.0 36.7 jit_solution(8940125172414596304)
XLA Ops:
  0.7 35.4 %shard_map.55 = f32[3,2,32,128]{3,2,1,0:T(8,128)S(1)} custom-call(bf16[3,2,4,8,2048]{4,3,2,1,0:T(8,128)(2,1)} %bitcast.4, s32[1,48]{1,0:T(1,128)} %bitcast.6, s32[1,48]{1,0:T(1,128)} %bitcast.7, s32[2,48]{1,0:T(2,128)} %bitcast.5, s32[1]{0:T(128)S(6)} %copy.7.counts), custom_call_target="tpu_custom_call" | custom-call | tf_op jit(solution)/shard_map/pallas_call | solution.py:386
  36.0 0.6 %copy.8 = f32[3,2,32,128]{3,2,1,0:T(8,128)} copy(f32[3,2,32,128]{3,2,1,0:T(8,128)S(1)} %shard_map.55) | data formatting | bytes 196608

commit v6 on v5

--- a/solution.py
+++ b/solution.py
@@ -192,12 +192,15 @@
         at = lax.rem(row + (ROWS - FIRST), ROWS)
         return (at & HALF) + ((at + me) & (HALF - 1))
 
-    def windows(row):
+    def windows(row, count=2):
         w = weights[...]
         for l in range(LOOKS):
-            g = [grams[row + k, l * IMGS : (l + 1) * IMGS, :] for k in range(5)]
+            g = [grams[row + k, l * IMGS : (l + 1) * IMGS, :] for k in range(3 + count)]
             middle = g[1] + g[2]
-            for k, box in enumerate((g[0] + middle + g[3], middle + (g[3] + g[4]))):
+            boxes = [g[0] + middle + g[3]]
+            if count == 2:
+                boxes.append(middle + (g[3] + g[4]))
+            for k, box in enumerate(boxes):
                 powers = along[row + k, l : l + 1] * across[row + k, :, l * 128 : (l + 1) * 128]
                 scaled = box * lax.rsqrt(powers + EPS) * w
                 sums[place(row + k), l : l + 1, :] = jnp.sum(scaled, axis=0, keepdims=True)
@@ -282,8 +285,9 @@
         to_up.start()
 
     rows_of(0)
-    spread([2, 3, 4, 5])
+    spread([2, 3, 4, 5, 6])
     pairs(2, 2)
+    windows(6, 1)
 
     @pl.when(has_up)
     def _():
@@ -310,8 +314,8 @@
 
     arrive(1)
     rows_of(1)
-    spread([6, 7, 8, 9, 10, 11, 12, 13])
-    pairs(6, 4)
+    spread([7, 8, 9, 10, 11, 12, 13, 14])
+    pairs(7, 4)
 
     goal, source = iota((128, 384), 0), iota((128, 384), 1) & 127
     q = goal & 7
@@ -357,10 +361,11 @@
     arrive(2)
     give(1)
     rows_of(2)
-    spread([14, 15, 16, 17, 18, 19])
-    spread([20, 21, 22, 23, 24, 25])
-    for row in range(14, 26, 2):
+    spread([15, 16, 17, 18, 19, 20])
+    spread([21, 22, 23, 24, 25])
+    for row in range(15, 25, 2):
         windows(row)
+    windows(25, 1)
     turn(0)
     give(0)
 

time: 36.8 us -> 36.7 us (level)
  no operation moved by 1% of the time
where the time goes in v6:
time: 36.7 us
  Pallas kernels  35.4 us (96%)
  between operations  0.66 us (2%)
  local copies, waits for them, and re-layouts  0.64 us (2%)
    pallas_call x1, Pallas kernels, body(): pl.pallas_call(kernel, out_shape=jax.ShapeDtypeStruct((OWN, 2, ROWS, 128)...  35.4 us

profile of v6, /device:TPU:1, one launch (start us, length us, event | category | flops | bytes accessed | tf_op | source)
XLA Modules:
  0.0 36.7 jit_solution(18395936298477159079)
XLA Ops:
  0.7 35.4 %shard_map.55 = f32[3,2,32,128]{3,2,1,0:T(8,128)S(1)} custom-call(bf16[3,2,4,8,2048]{4,3,2,1,0:T(8,128)(2,1)} %bitcast.4, s32[1,48]{1,0:T(1,128)} %bitcast.6, s32[1,48]{1,0:T(1,128)} %bitcast.7, s32[2,48]{1,0:T(2,128)} %bitcast.5, s32[1]{0:T(128)S(6)} %copy.7.counts), custom_call_target="tpu_custom_call" | custom-call | tf_op jit(solution)/shard_map/pallas_call | solution.py:391
  36.0 0.6 %copy.8 = f32[3,2,32,128]{3,2,1,0:T(8,128)} copy(f32[3,2,32,128]{3,2,1,0:T(8,128)S(1)} %shard_map.55) | data formatting | bytes 196608
